TPU v7x, 32 devices: a whole 2x2x4 slice. The times are simulated.
32 devices in a mesh: tp: 16 (over z, y, core), dp: 2 (over x).
Axes of the slice: x: 2, y: 2, z: 4, core: 2. Of those that a mesh axis runs over, the one named last changes fastest.
Arguments:
- tokens: bfloat16 [512, 8192], P('dp', 'tp'), parts along dimension 0, may hold values from -6 to 6
- grad_out: bfloat16 [512, 8192], P('dp', 'tp'), parts along dimension 0, may hold values from -6 to 6
- gate_blocks: bfloat16 [8192, 128, 128], P('tp'), may hold values from -0.09375 to 0.09375
- gate_index: int32 [128, 64], P('tp'), may hold values from 0 to 63, as said below
- gate_count: int32 [128], P('tp'), may hold values from 16 to 64, as said below
- up_blocks: bfloat16 [8192, 128, 128], P('tp'), may hold values from -0.09375 to 0.09375
- up_index: int32 [128, 64], P('tp'), may hold values from 0 to 63, as said below
- up_count: int32 [128], P('tp'), may hold values from 16 to 64, as said below
- down_blocks: bfloat16 [8192, 128, 128], P('tp'), may hold values from -0.0625 to 0.0625
- down_index: int32 [128, 64], P('tp'), may hold values from 0 to 63, as said below
- down_count: int32 [128], P('tp'), may hold values from 16 to 64, as said below
Outputs:
- outputs: bfloat16 [512, 8192], P('dp', 'tp'), parts along dimension 0
- grad_tokens: bfloat16 [512, 8192], P('dp', 'tp'), parts along dimension 0
There are 2 independent parts, one for each index of `dp`. A program takes and returns all parts, laid end to end along the dimension named above; an argument that names none is the same for every part. Nothing has to cross between parts.
Inputs may be any that keep to these rules, and one draw needn't show every extreme that they name: `gate_index`: each row is an ordering of the 64 block rows; entries at positions from gate_count onward are ignored. `gate_count`: both ends occur. `up_index`: each row is an ordering of the 64 block rows; entries at positions from up_count onward are ignored. `up_count`: both ends occur. `down_index`: each row is an ordering of the 64 block columns; entries at positions from down_count onward are ignored. `down_count`: both ends occur.
All inputs are finite; a program needn't handle non-finite values.
Results may differ from a plain program's by a relative error of at most 0.005.
Values may be sent and summed in bfloat16 or wider, within the bound.
A program may use at most 192 MiB of HBM per device.

v0:
```python
import jax
import jax.numpy as jnp
from jax import lax
from jax.sharding import PartitionSpec as P


def densify(blocks, index, count):
    hidden_blocks, slots = index.shape
    block = blocks.shape[-1]
    live = lax.broadcasted_iota(jnp.int32, (hidden_blocks, slots), 1) < count[:, None]
    places = lax.broadcasted_iota(jnp.int32, (hidden_blocks, slots, slots), 2)
    onehot = ((index[:, :, None] == places) & live[:, :, None]).astype(jnp.bfloat16)
    shaped = blocks.reshape(hidden_blocks, slots, block, block)
    return jnp.einsum("hsr,hsab->hrab", onehot, shaped, preferred_element_type=jnp.float32).astype(
        jnp.bfloat16
    )


def column_matrix(dense):
    hidden_blocks, slots, block, _ = dense.shape
    return dense.transpose(1, 2, 0, 3).reshape(slots * block, hidden_blocks * block)


def row_matrix(dense):
    hidden_blocks, slots, block, _ = dense.shape
    return dense.transpose(0, 2, 1, 3).reshape(hidden_blocks * block, slots * block)


def contract_last(left, right):
    return lax.dot_general(
        left, right, (((1,), (1,)), ((), ())), preferred_element_type=jnp.float32
    )


def body(
    tokens,
    grad_out,
    gate_blocks,
    gate_index,
    gate_count,
    up_blocks,
    up_index,
    up_count,
    down_blocks,
    down_index,
    down_count,
):
    hidden_blocks, slots = gate_index.shape
    block = gate_blocks.shape[-1]
    width = hidden_blocks * block
    gate_weight = column_matrix(densify(gate_blocks, gate_index, gate_count))
    up_weight = column_matrix(densify(up_blocks, up_index, up_count))
    down_weight = row_matrix(densify(down_blocks, down_index, down_count))
    all_tokens = lax.all_gather(tokens, "tp", axis=1, tiled=True)
    projected = jnp.concatenate(
        [
            jnp.dot(all_tokens, gate_weight, preferred_element_type=jnp.float32),
            jnp.dot(all_tokens, up_weight, preferred_element_type=jnp.float32),
        ],
        axis=1,
    )
    gate = projected[:, :width]
    upper = projected[:, width:]
    hidden = (gate * jax.nn.sigmoid(gate) * upper).astype(jnp.bfloat16)
    outputs = lax.psum_scatter(
        jnp.dot(hidden, down_weight, preferred_element_type=jnp.float32),
        "tp",
        scatter_dimension=1,
        tiled=True,
    )
    all_grads = lax.all_gather(grad_out, "tp", axis=1, tiled=True)
    grad_hidden = contract_last(all_grads, down_weight)
    gate = projected[:, :width]
    upper = projected[:, width:]
    sigma = jax.nn.sigmoid(gate)
    grad_gate = (grad_hidden * upper * sigma * (1.0 + gate * (1.0 - sigma))).astype(jnp.bfloat16)
    grad_up = (grad_hidden * gate * sigma).astype(jnp.bfloat16)
    grad_gate, grad_up = (grad_gate, grad_up)
    grad_tokens = lax.psum_scatter(
        contract_last(grad_gate, gate_weight) + contract_last(grad_up, up_weight),
        "tp",
        scatter_dimension=1,
        tiled=True,
    )
    return (outputs.astype(jnp.bfloat16), grad_tokens.astype(jnp.bfloat16))


def solution(mesh):
    placed = (
        P("dp", "tp"),
        P("dp", "tp"),
        P("tp", None, None),
        P("tp", None),
        P("tp"),
        P("tp", None, None),
        P("tp", None),
        P("tp"),
        P("tp", None, None),
        P("tp", None),
        P("tp"),
    )
    return jax.shard_map(
        body, mesh=mesh, in_specs=placed, out_specs=(P("dp", "tp"), P("dp", "tp")), check_vma=False
    )
```

profile of v0, /device:TPU:0, one launch (start us, length us, event | category | flops | bytes accessed | tf_op | source)
XLA Modules:
  0.0 382.0 jit_solution(13488214536210821447)
XLA Ops:
  7.2 0.0 all-gather.3.cloned.1.call-start
  7.2 0.7 all-gather.3.cloned.1.call-update
  7.9 0.0 all-gather.5.cloned.1.call-start
  7.9 0.7 all-gather.5.cloned.1.call-update
  8.6 0.0 reduce-scatter.3.cloned.1.call-start
  8.7 0.7 iota_compare_fusion.4
  9.4 22.9 %convert_bitcast_fusion = bf16[64,128,8,128]{3,0,1,2:T(8,128)(2,1)} fusion(bf16[8,64,128,128]{3,2,1,0:T(8,128)(2,1)} %bitcast.61, s32[8,64]{1,0:T(8,128)} %param.17, pred[8,64]{1,0:T(8,128)(4,1)S(1)} %iota_compare_fusion.4), kind=kOutput, calls=%fused_computation.18 | convolution fusion | flops 1082195968 | bytes 33556992 | tf_op jit(solution)/shard_map/hsr,hsab->hrab/dot_general | solution.py:14
  32.4 0.0 copy-done.3
  32.4 0.1 iota_compare_fusion.5
  32.4 18.6 %copy.19 = bf16[64,128,8,128]{3,2,1,0:T(8,128)(2,1)} copy(bf16[64,128,8,128]{3,0,1,2:T(8,128)(2,1)} %convert_bitcast_fusion) | data formatting | bytes 33554432 | tf_op jit(solution)/shard_map/convert_element_type | solution.py:14
  51.0 0.0 copy-done
  51.0 23.1 %convert_bitcast_fusion.1 = bf16[64,128,8,128]{3,0,1,2:T(8,128)(2,1)} fusion(bf16[8,64,128,128]{3,2,1,0:T(8,128)(2,1)} %bitcast.62, s32[8,64]{1,0:T(8,128)S(1)} %copy-done, pred[8,64]{1,0:T(8,128)(4,1)S(1)} %iota_compare_fusion.5), kind=kOutput, calls=%fused_computation.19 | convolution fusion | flops 1082195968 | bytes 33556992 | tf_op jit(solution)/shard_map/hsr,hsab->hrab/dot_general | solution.py:14
  74.2 18.6 %copy.17 = bf16[64,128,8,128]{3,2,1,0:T(8,128)(2,1)} copy(bf16[64,128,8,128]{3,0,1,2:T(8,128)(2,1)} %convert_bitcast_fusion.1) | data formatting | bytes 33554432 | tf_op jit(solution)/shard_map/convert_element_type | solution.py:14
  92.8 0.0 copy-done.4
  92.8 0.1 iota_compare_fusion.3
  92.9 0.0 copy-done.1
  92.9 23.8 %fusion.31 = bf16[8,64,128,128]{3,1,2,0:T(8,128)(2,1)} fusion(bf16[8,64,128,128]{3,2,1,0:T(8,128)(2,1)} %bitcast.63, s32[8,64]{1,0:T(8,128)S(1)} %copy-done.1, pred[8,64]{1,0:T(8,128)(4,1)S(1)} %iota_compare_fusion.3), kind=kOutput, calls=%fused_computation.27 | convolution fusion | flops 1082195968 | bytes 33556992 | tf_op jit(solution)/shard_map/hsr,hsab->hrab/dot_general | solution.py:14
  116.7 12.0 %fusion.37 = f32[256,1024]{0,1:T(8,128)S(1)} fusion(bf16[256,8192]{1,0:T(8,128)(2,1)} %all-gather.3.cloned.1.call-done, bf16[1024,8,8,128]{3,2,1,0:T(8,128)(2,1)} %bitcast.64), kind=kOutput, calls=%fused_computation.29 | convolution fusion | flops 4294967296 | bytes 22020096 | tf_op jit(solution)/shard_map/dot_general | solution.py:58
  128.7 0.0 copy-done.2
  128.7 8.5 %fusion.34 = f32[256,1024]{0,1:T(8,128)S(1)} fusion(bf16[256,8192]{1,0:T(8,128)(2,1)S(1)} %copy-done.2, bf16[1024,8,8,128]{3,2,1,0:T(8,128)(2,1)} %bitcast.66), kind=kOutput, calls=%fused_computation.28 | convolution fusion | flops 4294967296 | bytes 22020096 | tf_op jit(solution)/shard_map/dot_general | solution.py:57
  137.2 20.2 %fusion.2 = f32[256,8192]{1,0:T(8,128)} fusion(bf16[128,8,64,128]{3,2,1,0:T(8,128)(2,1)} %bitcast.68, f32[256,1024]{0,1:T(8,128)S(1)} %fusion.37, f32[256,1024]{0,1:T(8,128)S(1)} %fusion.34), kind=kOutput, calls=%fused_computation.2 | convolution fusion | flops 4296540160 | bytes 27262976 | tf_op jit(solution)/shard_map/dot_general | solution.py:66
  157.4 0.0 reduce-scatter.3.cloned.1.call-update
  157.4 0.0 reduce-scatter.5.cloned.1.call-start
  157.5 0.0 all-gather.5.cloned.1.call-done
  157.5 18.1 %fusion.40 = f32[256,1024]{0,1:T(8,128)S(1)} fusion(bf16[256,8192]{1,0:T(8,128)(2,1)} %all-gather.5.cloned.1.call-done, bf16[128,8,64,128]{3,2,1,0:T(8,128)(2,1)} %bitcast.69), kind=kOutput, calls=%fused_computation.30 | convolution fusion | flops 4294967296 | bytes 22020096 | tf_op jit(solution)/shard_map/dot_general | solution.py:30
  175.6 15.1 %fusion.4 = f32[256,8192]{1,0:T(8,128)} fusion(bf16[1024,8,8,128]{3,2,1,0:T(8,128)(2,1)} %bitcast.65, f32[256,1024]{0,1:T(8,128)S(1)} %fusion.40, f32[256,1024]{0,1:T(8,128)S(1)} %fusion.34), kind=kOutput, calls=%fused_computation.4 | convolution fusion | flops 4296540160 | bytes 27262976 | tf_op jit(solution)/shard_map/dot_general | solution.py:30
  190.7 17.1 %fusion.24 = f32[256,8192]{1,0:T(8,128)} fusion(f32[256,8192]{1,0:T(8,128)} %fusion.4, bf16[1024,8,8,128]{3,2,1,0:T(8,128)(2,1)} %bitcast.67, f32[256,1024]{0,1:T(8,128)S(1)} %fusion.34, f32[256,1024]{0,1:T(8,128)S(1)} %fusion.40, f32[256,1024]{0,1:T(8,128)S(1)} %fusion.37), kind=kOutput, calls=%fused_computation.26 | convolution fusion | flops 4299685888 | bytes 36700160 | tf_op jit(solution)/shard_map/dot_general | solution.py:30
  207.7 0.0 reduce-scatter.5.cloned.1.call-update
  207.7 56.9 %reduce-scatter.3.cloned.1.call-done = f32[256,512]{1,0:T(8,128)} async-done(((f32[256,8192]{1,0:T(8,128)}), f32[256,512]{1,0:T(8,128)}) %reduce-scatter.3.cloned.1.call-update) | async-done | bytes 524304 | tf_op jit(solution)/shard_map/reduce_scatter | solution.py:65
  264.7 1.8 convert_element_type.46
  266.5 106.8 %reduce-scatter.5.cloned.1.call-done = f32[256,512]{1,0:T(8,128)} async-done(((f32[256,8192]{1,0:T(8,128)}), f32[256,512]{1,0:T(8,128)}) %reduce-scatter.5.cloned.1.call-update) | async-done | bytes 524304 | tf_op jit(solution)/shard_map/reduce_scatter | solution.py:79
  373.2 1.8 convert_element_type.49
  (6 shorter events, 0.0 us)
Async XLA Ops:
  7.2 109.5 %all-gather.3.cloned.1.call-start = ((), (), s32[]{:S(2)}) async-start(), calls=%async_computation.2 | async-start | bytes 4456448 | tf_op jit(solution)/shard_map/all_gather | solution.py:54
  7.9 149.6 %all-gather.5.cloned.1.call-start = ((), (), s32[]{:S(2)}) async-start(), calls=%async_computation.4 | async-start | bytes 4456448 | tf_op jit(solution)/shard_map/all_gather | solution.py:71
  8.6 256.0 %reduce-scatter.3.cloned.1.call-start = ((), (), s32[]{:S(2)}) async-start(), calls=%async_computation.3 | async-start | bytes 8912896 | tf_op jit(solution)/shard_map/reduce_scatter | solution.py:65
  9.4 22.9 %copy-start.3 = (s32[8]{0:T(128)S(1)}, s32[8]{0:T(128)}, u32[]{:S(2)}) copy-start(s32[8]{0:T(128)} %param.15) | copy-start | bytes 100
  32.4 18.6 %copy-start = (s32[8,64]{1,0:T(8,128)S(1)}, s32[8,64]{1,0:T(8,128)}, u32[]{:S(2)}) copy-start(s32[8,64]{1,0:T(8,128)} %param.14) | copy-start | bytes 6148
  74.2 18.6 %copy-start.4 = (s32[8]{0:T(128)S(1)}, s32[8]{0:T(128)}, u32[]{:S(2)}) copy-start(s32[8]{0:T(128)} %param.21) | copy-start | bytes 100
  74.2 18.7 %copy-start.1 = (s32[8,64]{1,0:T(8,128)S(1)}, s32[8,64]{1,0:T(8,128)}, u32[]{:S(2)}) copy-start(s32[8,64]{1,0:T(8,128)} %param.20) | copy-start | bytes 6148
  116.6 12.0 %copy-start.2 = (bf16[256,8192]{1,0:T(8,128)(2,1)S(1)}, bf16[256,8192]{1,0:T(8,128)(2,1)}, u32[]{:S(2)}) copy-start(bf16[256,8192]{1,0:T(8,128)(2,1)} %all-gather.3.cloned.1.call-done) | copy-start | bytes 12582916
  157.4 215.8 %reduce-scatter.5.cloned.1.call-start = ((), (), s32[]{:S(2)}) async-start(), calls=%async_computation.5 | async-start | bytes 8912896 | tf_op jit(solution)/shard_map/reduce_scatter | solution.py:79
Sparse Core Ops, SparseCore 0:
  10.2 55.9 all-gather.2
  68.3 51.3 all-gather.4
  157.5 107.0 reduce-scatter.2
  268.6 104.5 reduce-scatter.4
where the time goes:
time: 389 us; the launch traced here: 382 us
  waiting for transfers between devices  165 us (42%)
  matrix products  161 us (41%)
  local copies, waits for them, and re-layouts  37.2 us (10%)
  between operations  14.2 us (4%)
  other arithmetic  4.42 us (1%)
    reduce_scatter x1, waiting for transfers between devices, body(): lax.psum_scatter(contract_last(grad_gate, gate_weight) + contract_last(gr...  107 us
    dot_general x3, matrix products, densify(): jnp.einsum('hsr,hsab->hrab', onehot, shaped, preferred_element_type=jnp.f...  69.8 us
    reduce_scatter x1, waiting for transfers between devices, body(): lax.psum_scatter(jnp.dot(hidden, down_weight, preferred_element_type=jnp....  56.9 us
    dot_general x3, matrix products, contract_last(): lax.dot_general(left, right, (((1,), (1,)), ((), ())), preferred_element_...  50.2 us
    convert_element_type x2, local copies, waits for them, and re-layouts, densify(): jnp.einsum('hsr,hsab->hrab', onehot, shaped, preferred_element_type=jnp.f...  37.2 us
    dot_general x1, matrix products, body(): jnp.dot(hidden, down_weight, preferred_element_type=jnp.float32)  20.2 us
    dot_general x1, matrix products, body(): jnp.dot(all_tokens, up_weight, preferred_element_type=jnp.float32)  12 us
    dot_general x1, matrix products, body(): jnp.dot(all_tokens, gate_weight, preferred_element_type=jnp.float32)  8.5 us
  transfers between devices with their start and end apart: 4, of which 2 were waited for; matrix products, arithmetic and copies ran while one was open for 53% of the time, Pallas kernels for 0%

commit v1 on v0

--- a/solution.py
+++ b/solution.py
@@ -1,7 +1,450 @@
+import functools
+
 import jax
 import jax.numpy as jnp
 from jax import lax
+from jax.experimental import pallas as pl
+from jax.experimental.pallas import tpu as pltpu
 from jax.sharding import PartitionSpec as P
+
+
+MESH = pl.DeviceIdType.MESH
+CORES = 2
+ROWS = 2
+VMEM_LIMIT = 60 * 1024 * 1024
+
+
+def places(index, count):
+    hidden_blocks, slots = index.shape
+    slot = lax.broadcasted_iota(jnp.int32, (hidden_blocks, slots, slots), 1)
+    place = lax.broadcasted_iota(jnp.int32, (hidden_blocks, slots, slots), 2)
+    where = jnp.sum(jnp.where(index[:, :, None] == place, slot, 0), axis=1)
+    base = lax.broadcasted_iota(jnp.int32, (hidden_blocks, slots), 0) * slots
+    return jnp.where(where < count[:, None], base + where, hidden_blocks * slots)
+
+
+def position(depth):
+    me = lax.axis_index("tp")
+    core = lax.rem(me, CORES)
+    row = lax.rem(me // CORES, ROWS)
+    layer = me // (CORES * ROWS)
+    return me, layer, row, core
+
+
+def shard_of(layer, row, core):
+    return (layer * ROWS + row) * CORES + core
+
+
+def greet(depth):
+    me, layer, row, core = position(depth)
+    barrier = pltpu.get_barrier_semaphore()
+    partners = [shard_of(layer, row, 1 - core), shard_of(layer, 1 - row, core)]
+    partners += [shard_of(lax.rem(layer + k, depth), row, core) for k in range(1, depth)]
+    for partner in partners:
+        pl.semaphore_signal(barrier, inc=1, device_id={"tp": partner}, device_id_type=MESH)
+    pl.semaphore_wait(barrier, len(partners))
+
+
+def remote(src, dst, send, recv, target):
+    return pltpu.make_async_remote_copy(
+        src_ref=src,
+        dst_ref=dst,
+        send_sem=send,
+        recv_sem=recv,
+        device_id={"tp": target},
+        device_id_type=MESH,
+    )
+
+
+def load_copies(hbm, buffer, sems, hidden_blocks, slots):
+    return [
+        pltpu.make_async_copy(
+            hbm.at[pl.ds(h * slots, slots)], buffer.at[pl.ds(h * slots, slots)], sems.at[h]
+        )
+        for h in range(hidden_blocks)
+    ]
+
+
+class Gather:
+    def __init__(self, depth, full, sems):
+        self.depth, self.full = depth, full
+        self.z_send, self.z_recv, self.y_send, self.y_recv, self.c_send, self.c_recv = sems
+        self.me, self.layer, self.row, self.core = position(depth)
+
+    def back(self, k):
+        return lax.rem(self.layer - k + self.depth, self.depth)
+
+    def z(self, k, shard):
+        target = shard_of(lax.rem(self.layer + k, self.depth), self.row, self.core)
+        block = self.full.at[shard]
+        return remote(block, block, self.z_send.at[k], self.z_recv.at[k], target)
+
+    def y(self, k, shard):
+        block = self.full.at[shard]
+        target = shard_of(self.layer, 1 - self.row, self.core)
+        return remote(block, block, self.y_send.at[k], self.y_recv.at[k], target)
+
+    def c(self, k, shard):
+        block = self.full.at[shard]
+        target = shard_of(self.layer, self.row, 1 - self.core)
+        return remote(block, block, self.c_send.at[k], self.c_recv.at[k], target)
+
+    def start_layers(self):
+        for k in range(1, self.depth):
+            self.z(k, self.me).start()
+
+    def start_own(self):
+        self.y(0, self.me).start()
+        self.c(0, self.me).start()
+
+    def from_layer(self, k):
+        shard = shard_of(self.back(k), self.row, self.core)
+        self.z(k, shard).wait_recv()
+        self.y(k, shard).start()
+        self.c(k, shard).start()
+
+    def from_row(self, k):
+        shard = shard_of(self.back(k), 1 - self.row, self.core)
+        self.y(k, shard).wait_recv()
+        self.c(self.depth + k, shard).start()
+
+    def chip_own(self, k):
+        self.c(k, shard_of(self.back(k), self.row, 1 - self.core)).wait_recv()
+        return self.back(k) * ROWS + self.row
+
+    def chip_other(self, k):
+        self.c(self.depth + k, shard_of(self.back(k), 1 - self.row, 1 - self.core)).wait_recv()
+        return self.back(k) * ROWS + 1 - self.row
+
+    def finish(self):
+        for k in range(1, self.depth):
+            self.z(k, self.me).wait_send()
+        for k in range(self.depth):
+            self.y(k, self.me).wait_send()
+        for k in range(2 * self.depth):
+            self.c(k, self.me).wait_send()
+
+
+def each(low, high, step):
+    def run(k, carry):
+        step(k)
+        return carry
+
+    lax.fori_loop(low, high, run, 0)
+
+
+def dot(left, right, contract=0):
+    return lax.dot_general(
+        left, right, (((1,), (contract,)), ((), ())), preferred_element_type=jnp.float32
+    )
+
+
+def first_kernel(depth, hidden_blocks, slots, block, *refs):
+    (tokens, grads, at_gate, at_up, at_down, gate_hbm, up_hbm, down_hbm) = refs[:8]
+    (hidden, grad_gate, grad_up) = refs[8:11]
+    (first, second, all_tokens, all_grads, projected, grad_hidden, load_sems) = refs[11:18]
+    token_sems, grad_sems = refs[18:24], refs[24:30]
+    me = position(depth)[0]
+    per_chip = slots // (depth * ROWS)
+    loads = load_copies(gate_hbm, first, load_sems.at[0], hidden_blocks, slots)
+    loads += load_copies(up_hbm, second, load_sems.at[1], hidden_blocks, slots)
+    down_loads = load_copies(down_hbm, first, load_sems.at[2], hidden_blocks, slots)
+    for load in loads:
+        load.start()
+    all_tokens[me] = tokens[...]
+    all_grads[me] = grads[...]
+    greet(depth)
+    tok = Gather(depth, all_tokens, token_sems)
+    grd = Gather(depth, all_grads, grad_sems)
+    tok.start_layers()
+    tok.start_own()
+    grd.start_own()
+    first[hidden_blocks * slots] = jnp.zeros((block, block), first.dtype)
+    second[hidden_blocks * slots] = jnp.zeros((block, block), second.dtype)
+    projected[...] = jnp.zeros_like(projected)
+    grad_hidden[...] = jnp.zeros_like(grad_hidden)
+    for load in loads:
+        load.wait()
+
+    def pair(full, chip):
+        return jnp.concatenate([full[CORES * chip + i] for i in range(CORES)], axis=1)
+
+    def project(chip):
+        def one(h):
+            rows = [
+                jnp.concatenate(
+                    [first[at_gate[h, chip * per_chip + j]], second[at_up[h, chip * per_chip + j]]], axis=1
+                )
+                for j in range(per_chip)
+            ]
+            projected[h] += dot(pair(all_tokens, chip), jnp.concatenate(rows, axis=0))
+
+        each(0, hidden_blocks, one)
+
+    def push_back(chip):
+        def one(p):
+            rows = [
+                jnp.concatenate(
+                    [first[at_down[2 * p + i, chip * per_chip + j]] for j in range(per_chip)], axis=1
+                )
+                for i in range(2)
+            ]
+            grad_hidden[p] += dot(pair(all_grads, chip), jnp.concatenate(rows, axis=0), 1)
+
+        each(0, hidden_blocks // 2, one)
+
+    def run(gather, work, between):
+        def layer_step(k):
+            gather.from_layer(k)
+            gather.from_row(k - 1)
+            work(gather.chip_own(k - 1))
+
+        each(1, depth, layer_step)
+        between()
+        gather.from_row(depth - 1)
+        work(gather.chip_own(depth - 1))
+        each(0, depth, lambda k: work(gather.chip_other(k)))
+
+    run(tok, project, grd.start_layers)
+    for load in down_loads:
+        load.start()
+
+    def activate(h):
+        gate, up = projected[h][:, :block], projected[h][:, block:]
+        hidden[h] = (gate * jax.nn.sigmoid(gate) * up).astype(hidden.dtype)
+
+    each(0, hidden_blocks, activate)
+    for load in down_loads:
+        load.wait()
+    run(grd, push_back, lambda: None)
+
+    def back(p):
+        for i in range(2):
+            h = 2 * p + i
+            gate, up = projected[h][:, :block], projected[h][:, block:]
+            flow = grad_hidden[p][:, i * block : (i + 1) * block]
+            sigma = jax.nn.sigmoid(gate)
+            grad_gate[h] = (flow * up * sigma * (1.0 + gate * (1.0 - sigma))).astype(grad_gate.dtype)
+            grad_up[h] = (flow * gate * sigma).astype(grad_up.dtype)
+
+    each(0, hidden_blocks // 2, back)
+    tok.finish()
+    grd.finish()
+
+
+class Scatter:
+    def __init__(self, depth, partial, held, bufs):
+        self.depth, self.partial, self.held = depth, partial, held
+        (self.c_out, self.c_in, self.y_out, self.y_in, self.z_out, self.z_in) = bufs[:6]
+        (self.c_send, self.c_recv, self.y_send, self.y_recv, self.z_send, self.z_recv) = bufs[6:]
+        self.me, self.layer, self.row, self.core = position(depth)
+
+    def ahead(self, k):
+        return lax.rem(self.layer + k, self.depth)
+
+    def c(self, i):
+        target = shard_of(self.layer, self.row, 1 - self.core)
+        return remote(self.c_out.at[i], self.c_in.at[i], self.c_send.at[i], self.c_recv.at[i], target)
+
+    def y(self, k):
+        target = shard_of(self.layer, 1 - self.row, self.core)
+        return remote(self.y_out.at[k], self.y_in.at[k], self.y_send.at[k], self.y_recv.at[k], target)
+
+    def z(self, k):
+        target = shard_of(self.ahead(k), self.row, self.core)
+        return remote(self.z_out.at[k], self.z_in.at[k], self.z_send.at[k], self.z_recv.at[k], target)
+
+    def sibling(self, k, other):
+        row = 1 - self.row if other else self.row
+        i = k if other else self.depth + k
+        for cols, value in self.partial(shard_of(self.ahead(k), row, 1 - self.core)):
+            self.c_out[i, :, cols] = value.astype(self.c_out.dtype)
+        self.c(i).start()
+
+    def across(self, k):
+        parts = self.partial(shard_of(self.ahead(k), 1 - self.row, self.core))
+        self.c(k).wait_recv()
+        for cols, value in parts:
+            total = value + self.c_in[k, :, cols].astype(jnp.float32)
+            self.y_out[k, :, cols] = total.astype(self.y_out.dtype)
+        self.y(k).start()
+
+    def keep(self, k):
+        parts = self.partial(shard_of(self.ahead(k), self.row, self.core))
+        self.c(self.depth + k).wait_recv()
+        for cols, value in parts:
+            self.held[k, :, cols] = value + self.c_in[self.depth + k, :, cols].astype(jnp.float32)
+
+    def along(self, k):
+        self.y(k).wait_recv()
+        total = self.held[k] + self.y_in[k].astype(jnp.float32)
+        self.z_out[k] = total.astype(self.z_out.dtype)
+        self.z(k).start()
+
+    def result(self, out):
+        self.y(0).wait_recv()
+        total = self.held[0] + self.y_in[0].astype(jnp.float32)
+        for k in range(1, self.depth):
+            self.z(k).wait_recv()
+            total = total + self.z_in[k].astype(jnp.float32)
+        out[...] = total.astype(out.dtype)
+
+    def finish(self):
+        for i in range(2 * self.depth):
+            self.c(i).wait_send()
+        for k in range(self.depth):
+            self.y(k).wait_send()
+        for k in range(1, self.depth):
+            self.z(k).wait_send()
+
+
+def second_kernel(depth, hidden_blocks, slots, block, *refs):
+    (hidden, grad_gate, grad_up, at_gate, at_up, at_down, gate_hbm, up_hbm, down_hbm) = refs[:9]
+    (outputs, grad_tokens) = refs[9:11]
+    (first, second, held_out, held_grad, load_sems) = refs[11:16]
+    out_bufs, grad_bufs = refs[16:28], refs[28:40]
+    per_shard = slots // (depth * ROWS * CORES)
+    down_loads = load_copies(down_hbm, first, load_sems.at[0], hidden_blocks, slots)
+    gate_loads = load_copies(gate_hbm, second, load_sems.at[1], hidden_blocks, slots)
+    up_loads = load_copies(up_hbm, first, load_sems.at[2], hidden_blocks, slots)
+    for load in down_loads + gate_loads:
+        load.start()
+    first[hidden_blocks * slots] = jnp.zeros((block, block), first.dtype)
+    second[hidden_blocks * slots] = jnp.zeros((block, block), second.dtype)
+    greet(depth)
+
+    def wide(ref):
+        return jnp.concatenate([ref[h] for h in range(hidden_blocks)], axis=1)
+
+    def out_partial(shard):
+        parts = []
+        for j in range(0, per_shard, 2):
+            place = shard * per_shard + j
+            rows = [
+                jnp.concatenate([first[at_down[h, place + i]] for i in range(2)], axis=1)
+                for h in range(hidden_blocks)
+            ]
+            value = dot(wide(hidden), jnp.concatenate(rows, axis=0))
+            parts.append((slice(j * block, (j + 2) * block), value))
+        return parts
+
+    def grad_partial(shard):
+        parts = []
+        for j in range(0, per_shard, 2):
+            place = shard * per_shard + j
+            value = None
+            for left, buffer, at in ((grad_gate, second, at_gate), (grad_up, first, at_up)):
+                rows = [
+                    jnp.concatenate([buffer[at[h, place + i]] for h in range(hidden_blocks)], axis=1)
+                    for i in range(2)
+                ]
+                term = dot(wide(left), jnp.concatenate(rows, axis=0), 1)
+                value = term if value is None else value + term
+            parts.append((slice(j * block, (j + 2) * block), value))
+        return parts
+
+    out = Scatter(depth, out_partial, held_out, out_bufs)
+    grad = Scatter(depth, grad_partial, held_grad, grad_bufs)
+    for load in down_loads:
+        load.wait()
+    each(0, depth, lambda k: out.sibling(k, True))
+    each(0, depth, out.across)
+    each(0, depth, lambda k: out.sibling(k, False))
+    each(0, depth, out.keep)
+    for load in up_loads:
+        load.start()
+    for load in gate_loads + up_loads:
+        load.wait()
+    each(0, depth, lambda k: grad.sibling(k, True))
+    each(0, depth, grad.across)
+    each(1, depth, out.along)
+    each(0, depth, lambda k: grad.sibling(k, False))
+    each(0, depth, grad.keep)
+    each(1, depth, grad.along)
+    out.result(outputs)
+    grad.result(grad_tokens)
+    out.finish()
+    grad.finish()
+
+
+def fused_body(depth, tokens, grad_out, gate_blocks, gate_index, gate_count, up_blocks, up_index, up_count, down_blocks, down_index, down_count):
+    hidden_blocks, slots = gate_index.shape
+    block = gate_blocks.shape[-1]
+    rows, shard = tokens.shape
+    devices = depth * ROWS * CORES
+    kind = tokens.dtype
+    at = [
+        places(gate_index, gate_count),
+        places(up_index, up_count),
+        places(down_index, down_count),
+    ]
+    vmem = pl.BlockSpec(memory_space=pltpu.VMEM)
+    smem = pl.BlockSpec(memory_space=pltpu.SMEM)
+    anywhere = pl.BlockSpec(memory_space=pl.ANY)
+    dma = pltpu.SemaphoreType.DMA
+    weights = pltpu.VMEM((hidden_blocks * slots + 1, block, block), gate_blocks.dtype)
+    gather_sems = [dma((n,)) for n in (depth, depth, depth, depth, 2 * depth, 2 * depth)]
+    thin = jax.ShapeDtypeStruct((hidden_blocks, rows, block), jnp.bfloat16)
+    flops = 2 * rows * shard * devices * hidden_blocks * block * 3
+    cost = pl.CostEstimate(flops=flops, bytes_accessed=3 * gate_blocks.size * 2, transcendentals=0)
+    hidden, grad_gate, grad_up = pl.pallas_call(
+        functools.partial(first_kernel, depth, hidden_blocks, slots, block),
+        out_shape=[thin] * 3,
+        in_specs=[vmem] * 2 + [smem] * 3 + [anywhere] * 3,
+        out_specs=[vmem] * 3,
+        scratch_shapes=[
+            weights,
+            weights,
+            pltpu.VMEM((devices, rows, shard), kind),
+            pltpu.VMEM((devices, rows, shard), kind),
+            pltpu.VMEM((hidden_blocks, rows, 2 * block), jnp.float32),
+            pltpu.VMEM((hidden_blocks // 2, rows, 2 * block), jnp.float32),
+            dma((3, hidden_blocks)),
+        ]
+        + gather_sems
+        + gather_sems,
+        compiler_params=pltpu.CompilerParams(
+            collective_id=0, has_side_effects=True, vmem_limit_bytes=VMEM_LIMIT
+        ),
+        cost_estimate=cost,
+        name="gather_and_project",
+    )(tokens, grad_out, *at, gate_blocks, up_blocks, down_blocks)
+    scatter_bufs = [
+        pltpu.VMEM((n, rows, shard), jnp.bfloat16)
+        for n in (2 * depth, 2 * depth, depth, depth, depth, depth)
+    ]
+    scatter_sems = [dma((n,)) for n in (2 * depth, 2 * depth, depth, depth, depth, depth)]
+    held = pltpu.VMEM((depth, rows, shard), jnp.float32)
+    result = jax.ShapeDtypeStruct((rows, shard), jnp.bfloat16)
+    return pl.pallas_call(
+        functools.partial(second_kernel, depth, hidden_blocks, slots, block),
+        out_shape=[result] * 2,
+        in_specs=[vmem] * 3 + [smem] * 3 + [anywhere] * 3,
+        out_specs=[vmem] * 2,
+        scratch_shapes=[weights, weights, held, held, dma((3, hidden_blocks))]
+        + (scatter_bufs + scatter_sems) * 2,
+        compiler_params=pltpu.CompilerParams(
+            collective_id=1, has_side_effects=True, vmem_limit_bytes=VMEM_LIMIT
+        ),
+        cost_estimate=cost,
+        name="expand_and_scatter",
+    )(hidden, grad_gate, grad_up, *at, gate_blocks, up_blocks, down_blocks)
+
+
+def fits(mesh, tokens, gate_index, gate_blocks):
+    tp, dp = mesh.shape["tp"], mesh.shape["dp"]
+    rows, shard = tokens.shape[0] // dp, tokens.shape[1] // tp
+    hidden_blocks, slots = gate_index.shape[0] // tp, gate_index.shape[1]
+    block = gate_blocks.shape[-1]
+    held = hidden_blocks * slots * block * block * 2 * 2 + 2 * rows * tokens.shape[1] * 5
+    return (
+        tp % (CORES * ROWS) == 0
+        and tp > CORES * ROWS
+        and shard % (2 * block) == 0
+        and hidden_blocks % 2 == 0
+        and rows % 16 == 0
+        and held <= VMEM_LIMIT
+    )
 
 
 def densify(blocks, index, count):
@@ -99,6 +542,14 @@
         P("tp", None),
         P("tp"),
     )
-    return jax.shard_map(
-        body, mesh=mesh, in_specs=placed, out_specs=(P("dp", "tp"), P("dp", "tp")), check_vma=False
-    )
+
+    def run(*args):
+        tokens, gate_blocks, gate_index = args[0], args[2], args[3]
+        inner = body
+        if fits(mesh, tokens, gate_index, gate_blocks):
+            inner = functools.partial(fused_body, mesh.shape["tp"] // (CORES * ROWS))
+        return jax.shard_map(
+            inner, mesh=mesh, in_specs=placed, out_specs=(P("dp", "tp"), P("dp", "tp")), check_vma=False
+        )(*args)
+
+    return run

time: 389 us -> 165 us (0.42); the launches traced: 382 us -> 163 us
  waiting for transfers between devices: 165 us -> 0 us
  matrix products: 161 us -> 0 us
  Pallas kernels: 0 us -> 156 us
  local copies, waits for them, and re-layouts: 37.2 us -> 3.34 us
  between operations: 14.2 us -> 0.66 us
    reduce_scatter x2 -> x0, waiting for transfers between devices: 164 us -> none  [the longest x1 107 us: body(): lax.psum_scatter(contract_last(grad_gate, gate_weight) + contract_last(gr...]
    dot_general x9 -> x0, matrix products: 161 us -> none  [the longest x3 69.8 us: densify(): jnp.einsum('hsr,hsab->hrab', onehot, shaped, preferred_element_type=jnp.f...]
    pallas_call x0 -> x2, Pallas kernels: none -> 156 us  [the longest x1 80.1 us: fused_body(): pl.pallas_call(functools.partial(first_kernel, depth, hidden_blocks, slot...]
    convert_element_type x2 -> x0, local copies, waits for them, and re-layouts: 37.2 us -> none  [densify(): jnp.einsum('hsr,hsab->hrab', onehot, shaped, preferred_element_type=jnp.f...]
  transfers between devices with their start and end apart: 4 -> 0, of which waited for: 2 -> 0; matrix products, arithmetic and copies ran while one was open for 53% -> 0% of each run, Pallas kernels for 0% -> 0%
where the time goes in v1:
time: 165 us; the launch traced here: 163 us
  Pallas kernels  156 us (95%)
  local copies, waits for them, and re-layouts  3.34 us (2%)
  other arithmetic  3.12 us (2%)
    pallas_call x1, Pallas kernels, fused_body(): pl.pallas_call(functools.partial(first_kernel, depth, hidden_blocks, slot...  80.1 us
    pallas_call x1, Pallas kernels, fused_body(): pl.pallas_call(functools.partial(second_kernel, depth, hidden_blocks, slo...  76.2 us
    unnamed x2, local copies, waits for them, and re-layouts  3.34 us

profile of v1, /device:TPU:0, one launch (start us, length us, event | category | flops | bytes accessed | tf_op | source)
XLA Modules:
  0.0 163.4 jit_solution(13885793600458962635)
XLA Ops:
  0.6 0.8 select_reduce_fusion.2
  1.5 0.9 select_reduce_fusion
  2.4 1.4 add_select_fusion
  3.8 80.1 %gather_and_project.1 = (bf16[8,256,128]{2,1,0:T(8,128)(2,1)}, bf16[8,256,128]{2,1,0:T(8,128)(2,1)}, bf16[8,256,128]{2,1,0:T(8,128)(2,1)}) custom-call(bf16[256,512]{1,0:T(8,128)(2,1)} %refs_0_.1, bf16[256,512]{1,0:T(8,128)(2,1)} %refs_1_.1, s32[8,64]{1,0:T(8,128)} %get-tuple-element.10.refs_2_.refs_3_, s32[8,64]{1,0:T(8,128)} %get-tuple-element.9.refs_3_.refs_4_, ...), custom_call_target="tpu_custom_call" | custom-call | flops 12884901888 | bytes 50331648 | tf_op jit(solution)/shard_map/gather_and_project/pallas_call | solution.py:390
  83.8 76.2 %expand_and_scatter.1 = (bf16[256,512]{1,0:T(8,128)(2,1)}, bf16[256,512]{1,0:T(8,128)(2,1)}) custom-call(bf16[8,256,128]{2,1,0:T(8,128)(2,1)} %get-tuple-element.5.refs_0_, bf16[8,256,128]{2,1,0:T(8,128)(2,1)} %get-tuple-element.6.refs_1_, bf16[8,256,128]{2,1,0:T(8,128)(2,1)} %get-tuple-element.7.refs_2_, s32[8,64]{1,0:T(8,128)} %get-tuple-element.10.refs_2_.refs_3_, ...), custom_call_target="tpu_custom_call" | custom-call | flops 12884901888 | bytes 50331648 | tf_op jit(solution)/shard_map/expand_and_scatter/pallas_call | solution.py:419
  160.0 1.7 %copy.15 = bf16[256,512]{1,0:T(8,128)(2,1)} copy(bf16[256,512]{1,0:T(8,128)(2,1)} %get-tuple-element.15) | data formatting | bytes 524288
  161.7 1.7 %copy.16 = bf16[256,512]{1,0:T(8,128)(2,1)} copy(bf16[256,512]{1,0:T(8,128)(2,1)} %get-tuple-element.16) | data formatting | bytes 524288
  (1 shorter events, 0.0 us)

commit v2 on v1

--- a/solution.py
+++ b/solution.py
@@ -11,7 +11,7 @@
 MESH = pl.DeviceIdType.MESH
 CORES = 2
 ROWS = 2
-VMEM_LIMIT = 60 * 1024 * 1024
+VMEM_LIMIT = 63 * 1024 * 1024
 
 
 def places(index, count):
@@ -65,64 +65,78 @@
     ]
 
 
+def nearest(layer, depth, i):
+    both = jnp.minimum(layer, depth - 1 - layer)
+    down = jnp.where(2 * layer > depth - 1, layer - (i - both), layer + (i - both))
+    step = (i + 1) // 2
+    near = jnp.where(lax.rem(i, 2) == 1, layer - step, layer + step)
+    return jnp.where(i <= 2 * both, near, down)
+
+
 class Gather:
     def __init__(self, depth, full, sems):
         self.depth, self.full = depth, full
         self.z_send, self.z_recv, self.y_send, self.y_recv, self.c_send, self.c_recv = sems
         self.me, self.layer, self.row, self.core = position(depth)
 
-    def back(self, k):
-        return lax.rem(self.layer - k + self.depth, self.depth)
-
-    def z(self, k, shard):
-        target = shard_of(lax.rem(self.layer + k, self.depth), self.row, self.core)
-        block = self.full.at[shard]
-        return remote(block, block, self.z_send.at[k], self.z_recv.at[k], target)
-
-    def y(self, k, shard):
-        block = self.full.at[shard]
+    def at(self, i):
+        return nearest(self.layer, self.depth, jnp.int32(i))
+
+    def z(self, way, layer):
+        block = self.full.at[shard_of(layer, self.row, self.core)]
+        step = 1 if way == 0 else -1
+        target = shard_of(lax.rem(self.layer + step + self.depth, self.depth), self.row, self.core)
+        return remote(block, block, self.z_send.at[way, layer], self.z_recv.at[layer], target)
+
+    def y(self, layer, row):
+        block = self.full.at[shard_of(layer, row, self.core)]
         target = shard_of(self.layer, 1 - self.row, self.core)
-        return remote(block, block, self.y_send.at[k], self.y_recv.at[k], target)
-
-    def c(self, k, shard):
-        block = self.full.at[shard]
+        return remote(block, block, self.y_send.at[layer], self.y_recv.at[layer], target)
+
+    def c(self, layer, row, core):
+        block = self.full.at[shard_of(layer, row, core)]
         target = shard_of(self.layer, self.row, 1 - self.core)
-        return remote(block, block, self.c_send.at[k], self.c_recv.at[k], target)
-
-    def start_layers(self):
-        for k in range(1, self.depth):
-            self.z(k, self.me).start()
-
-    def start_own(self):
-        self.y(0, self.me).start()
-        self.c(0, self.me).start()
-
-    def from_layer(self, k):
-        shard = shard_of(self.back(k), self.row, self.core)
-        self.z(k, shard).wait_recv()
-        self.y(k, shard).start()
-        self.c(k, shard).start()
-
-    def from_row(self, k):
-        shard = shard_of(self.back(k), 1 - self.row, self.core)
-        self.y(k, shard).wait_recv()
-        self.c(self.depth + k, shard).start()
-
-    def chip_own(self, k):
-        self.c(k, shard_of(self.back(k), self.row, 1 - self.core)).wait_recv()
-        return self.back(k) * ROWS + self.row
-
-    def chip_other(self, k):
-        self.c(self.depth + k, shard_of(self.back(k), 1 - self.row, 1 - self.core)).wait_recv()
-        return self.back(k) * ROWS + 1 - self.row
+        i = row * self.depth + layer
+        return remote(block, block, self.c_send.at[i], self.c_recv.at[i], target)
+
+    def hop(self, layer, act):
+        @pl.when(jnp.logical_and(layer <= self.layer, self.layer < self.depth - 1))
+        def _():
+            act(self.z(0, layer))
+
+        @pl.when(jnp.logical_and(layer >= self.layer, self.layer > 0))
+        def _():
+            act(self.z(1, layer))
+
+    def spread(self, layer):
+        self.hop(layer, lambda copy: copy.start())
+        self.y(layer, self.row).start()
+        self.c(layer, self.row, self.core).start()
+
+    def from_layer(self, i):
+        layer = self.at(i)
+        self.z(0, layer).wait_recv()
+        self.spread(layer)
+
+    def from_row(self, i):
+        layer = self.at(i)
+        self.y(layer, 1 - self.row).wait_recv()
+        self.c(layer, 1 - self.row, self.core).start()
+
+    def chip(self, i, other):
+        layer = self.at(i)
+        row = 1 - self.row if other else self.row
+        self.c(layer, row, 1 - self.core).wait_recv()
+        return layer * ROWS + row
 
     def finish(self):
-        for k in range(1, self.depth):
-            self.z(k, self.me).wait_send()
-        for k in range(self.depth):
-            self.y(k, self.me).wait_send()
-        for k in range(2 * self.depth):
-            self.c(k, self.me).wait_send()
+        def one(layer):
+            self.hop(layer, lambda copy: copy.wait_send())
+            self.y(layer, self.row).wait_send()
+            for row in range(ROWS):
+                self.c(layer, row, self.core).wait_send()
+
+        each(0, self.depth, one)
 
 
 def each(low, high, step):
@@ -142,13 +156,13 @@
 def first_kernel(depth, hidden_blocks, slots, block, *refs):
     (tokens, grads, at_gate, at_up, at_down, gate_hbm, up_hbm, down_hbm) = refs[:8]
     (hidden, grad_gate, grad_up) = refs[8:11]
-    (first, second, all_tokens, all_grads, projected, grad_hidden, load_sems) = refs[11:18]
-    token_sems, grad_sems = refs[18:24], refs[24:30]
+    (first, second, third, all_tokens, all_grads, projected, grad_hidden, load_sems) = refs[11:19]
+    token_sems, grad_sems = refs[19:25], refs[25:31]
     me = position(depth)[0]
     per_chip = slots // (depth * ROWS)
     loads = load_copies(gate_hbm, first, load_sems.at[0], hidden_blocks, slots)
     loads += load_copies(up_hbm, second, load_sems.at[1], hidden_blocks, slots)
-    down_loads = load_copies(down_hbm, first, load_sems.at[2], hidden_blocks, slots)
+    down_loads = load_copies(down_hbm, third, load_sems.at[2], hidden_blocks, slots)
     for load in loads:
         load.start()
     all_tokens[me] = tokens[...]
@@ -156,15 +170,16 @@
     greet(depth)
     tok = Gather(depth, all_tokens, token_sems)
     grd = Gather(depth, all_grads, grad_sems)
-    tok.start_layers()
-    tok.start_own()
-    grd.start_own()
+    tok.spread(tok.layer)
     first[hidden_blocks * slots] = jnp.zeros((block, block), first.dtype)
     second[hidden_blocks * slots] = jnp.zeros((block, block), second.dtype)
+    third[hidden_blocks * slots] = jnp.zeros((block, block), third.dtype)
     projected[...] = jnp.zeros_like(projected)
     grad_hidden[...] = jnp.zeros_like(grad_hidden)
     for load in loads:
         load.wait()
+    for load in down_loads:
+        load.start()
 
     def pair(full, chip):
         return jnp.concatenate([full[CORES * chip + i] for i in range(CORES)], axis=1)
@@ -185,7 +200,7 @@
         def one(p):
             rows = [
                 jnp.concatenate(
-                    [first[at_down[2 * p + i, chip * per_chip + j]] for j in range(per_chip)], axis=1
+                    [third[at_down[2 * p + i, chip * per_chip + j]] for j in range(per_chip)], axis=1
                 )
                 for i in range(2)
             ]
@@ -193,30 +208,37 @@
 
         each(0, hidden_blocks // 2, one)
 
-    def run(gather, work, between):
-        def layer_step(k):
-            gather.from_layer(k)
-            gather.from_row(k - 1)
-            work(gather.chip_own(k - 1))
-
-        each(1, depth, layer_step)
-        between()
-        gather.from_row(depth - 1)
-        work(gather.chip_own(depth - 1))
-        each(0, depth, lambda k: work(gather.chip_other(k)))
-
-    run(tok, project, grd.start_layers)
-    for load in down_loads:
-        load.start()
-
     def activate(h):
         gate, up = projected[h][:, :block], projected[h][:, block:]
         hidden[h] = (gate * jax.nn.sigmoid(gate) * up).astype(hidden.dtype)
 
-    each(0, hidden_blocks, activate)
+    def arrive(gather, work):
+        gather.from_layer(1)
+        gather.from_row(0)
+        work(gather.chip(0, False))
+
+        def step(i):
+            gather.from_layer(i)
+            gather.from_row(i - 1)
+            work(gather.chip(i - 1, False))
+            work(gather.chip(i - 2, True))
+
+        each(2, depth, step)
+
+    arrive(tok, project)
+    grd.spread(grd.layer)
+    project(tok.chip(depth - 1, False))
+    project(tok.chip(depth - 2, True))
+    tok.from_row(depth - 1)
     for load in down_loads:
         load.wait()
-    run(grd, push_back, lambda: None)
+    project(tok.chip(depth - 1, True))
+    arrive(grd, push_back)
+    push_back(grd.chip(depth - 1, False))
+    push_back(grd.chip(depth - 2, True))
+    grd.from_row(depth - 1)
+    each(0, hidden_blocks, activate)
+    push_back(grd.chip(depth - 1, True))
 
     def back(p):
         for i in range(2):
@@ -239,63 +261,102 @@
         (self.c_send, self.c_recv, self.y_send, self.y_recv, self.z_send, self.z_recv) = bufs[6:]
         self.me, self.layer, self.row, self.core = position(depth)
 
-    def ahead(self, k):
-        return lax.rem(self.layer + k, self.depth)
+    def far(self, n):
+        return nearest(self.layer, self.depth, jnp.int32(self.depth - 1 - n))
 
     def c(self, i):
         target = shard_of(self.layer, self.row, 1 - self.core)
         return remote(self.c_out.at[i], self.c_in.at[i], self.c_send.at[i], self.c_recv.at[i], target)
 
-    def y(self, k):
+    def y(self, n):
+        layer = self.far(n)
         target = shard_of(self.layer, 1 - self.row, self.core)
-        return remote(self.y_out.at[k], self.y_in.at[k], self.y_send.at[k], self.y_recv.at[k], target)
-
-    def z(self, k):
-        target = shard_of(self.ahead(k), self.row, self.core)
-        return remote(self.z_out.at[k], self.z_in.at[k], self.z_send.at[k], self.z_recv.at[k], target)
-
-    def sibling(self, k, other):
+        return remote(
+            self.y_out.at[layer], self.y_in.at[layer], self.y_send.at[layer], self.y_recv.at[layer], target
+        )
+
+    def z(self, layer):
+        up = layer > self.layer
+        step = jnp.where(up, 1, -1)
+        neighbour = lax.rem(self.layer + step + self.depth, self.depth)
+        place = jnp.where(jnp.logical_and(layer == neighbour, step < 0), self.depth, layer)
+        target = shard_of(neighbour, self.row, self.core)
+        return remote(
+            self.z_out.at[layer], self.z_in.at[place], self.z_send.at[layer], self.z_recv.at[place], target
+        )
+
+    def arrival(self, place):
+        block = self.z_in.at[place]
+        target = shard_of(self.layer, self.row, 1 - self.core)
+        return remote(block, block, self.z_send.at[0], self.z_recv.at[place], target)
+
+    def sibling(self, n, other):
+        layer = self.far(n)
         row = 1 - self.row if other else self.row
-        i = k if other else self.depth + k
-        for cols, value in self.partial(shard_of(self.ahead(k), row, 1 - self.core)):
+        i = layer if other else self.depth + layer
+        for cols, value in self.partial(shard_of(layer, row, 1 - self.core)):
             self.c_out[i, :, cols] = value.astype(self.c_out.dtype)
         self.c(i).start()
 
-    def across(self, k):
-        parts = self.partial(shard_of(self.ahead(k), 1 - self.row, self.core))
-        self.c(k).wait_recv()
+    def across(self, n):
+        layer = self.far(n)
+        parts = self.partial(shard_of(layer, 1 - self.row, self.core))
+        self.c(layer).wait_recv()
         for cols, value in parts:
-            total = value + self.c_in[k, :, cols].astype(jnp.float32)
-            self.y_out[k, :, cols] = total.astype(self.y_out.dtype)
-        self.y(k).start()
-
-    def keep(self, k):
-        parts = self.partial(shard_of(self.ahead(k), self.row, self.core))
-        self.c(self.depth + k).wait_recv()
+            total = value + self.c_in[layer, :, cols].astype(jnp.float32)
+            self.y_out[layer, :, cols] = total.astype(self.y_out.dtype)
+
+    def send_row(self, n):
+        if n >= 2:
+            self.y(n - 2).wait_send()
+        self.y(n).start()
+
+    def keep(self, n):
+        layer = self.far(n)
+        parts = self.partial(shard_of(layer, self.row, self.core))
+        self.c(self.depth + layer).wait_recv()
         for cols, value in parts:
-            self.held[k, :, cols] = value + self.c_in[self.depth + k, :, cols].astype(jnp.float32)
-
-    def along(self, k):
-        self.y(k).wait_recv()
-        total = self.held[k] + self.y_in[k].astype(jnp.float32)
-        self.z_out[k] = total.astype(self.z_out.dtype)
-        self.z(k).start()
+            self.held[layer, :, cols] = value + self.c_in[self.depth + layer, :, cols].astype(jnp.float32)
+
+    def along(self, n):
+        layer = self.far(n)
+        self.y(n).wait_recv()
+        self.held[layer] = self.held[layer] + self.y_in[layer].astype(jnp.float32)
+        inner = jnp.logical_and(self.layer > 0, self.layer < self.depth - 1)
+
+        @pl.when(inner)
+        def _():
+            self.arrival(layer).wait_recv()
+            self.held[layer] = self.held[layer] + self.z_in[layer].astype(jnp.float32)
+
+        self.z_out[layer] = self.held[layer].astype(self.z_out.dtype)
+        self.z(layer).start()
 
     def result(self, out):
-        self.y(0).wait_recv()
-        total = self.held[0] + self.y_in[0].astype(jnp.float32)
-        for k in range(1, self.depth):
-            self.z(k).wait_recv()
-            total = total + self.z_in[k].astype(jnp.float32)
-        out[...] = total.astype(out.dtype)
+        last = self.depth - 1
+        self.y(last).wait_recv()
+        mine = self.layer
+        self.held[mine] = self.held[mine] + self.y_in[mine].astype(jnp.float32)
+
+        @pl.when(self.layer > 0)
+        def _():
+            self.arrival(mine).wait_recv()
+            self.held[mine] = self.held[mine] + self.z_in[mine].astype(jnp.float32)
+
+        @pl.when(self.layer < self.depth - 1)
+        def _():
+            self.arrival(self.depth).wait_recv()
+            self.held[mine] = self.held[mine] + self.z_in[self.depth].astype(jnp.float32)
+
+        out[...] = self.held[mine].astype(out.dtype)
 
     def finish(self):
         for i in range(2 * self.depth):
             self.c(i).wait_send()
-        for k in range(self.depth):
-            self.y(k).wait_send()
-        for k in range(1, self.depth):
-            self.z(k).wait_send()
+        for n in range(max(self.depth - 2, 0), self.depth):
+            self.y(n).wait_send()
+        for n in range(self.depth - 1):
+            self.z(self.far(n)).wait_send()
 
 
 def second_kernel(depth, hidden_blocks, slots, block, *refs):
@@ -307,7 +368,7 @@
     down_loads = load_copies(down_hbm, first, load_sems.at[0], hidden_blocks, slots)
     gate_loads = load_copies(gate_hbm, second, load_sems.at[1], hidden_blocks, slots)
     up_loads = load_copies(up_hbm, first, load_sems.at[2], hidden_blocks, slots)
-    for load in down_loads + gate_loads:
+    for load in down_loads:
         load.start()
     first[hidden_blocks * slots] = jnp.zeros((block, block), first.dtype)
     second[hidden_blocks * slots] = jnp.zeros((block, block), second.dtype)
@@ -347,21 +408,35 @@
     grad = Scatter(depth, grad_partial, held_grad, grad_bufs)
     for load in down_loads:
         load.wait()
-    each(0, depth, lambda k: out.sibling(k, True))
+    for load in gate_loads:
+        load.start()
+    each(0, depth, lambda n: out.sibling(n, True))
     each(0, depth, out.across)
-    each(0, depth, lambda k: out.sibling(k, False))
+    out.send_row(0)
+    out.send_row(1)
+    each(0, depth, lambda n: out.sibling(n, False))
     each(0, depth, out.keep)
     for load in up_loads:
         load.start()
     for load in gate_loads + up_loads:
         load.wait()
-    each(0, depth, lambda k: grad.sibling(k, True))
+    each(0, depth, lambda n: grad.sibling(n, True))
+    out.send_row(2)
+    out.along(0)
     each(0, depth, grad.across)
-    each(1, depth, out.along)
-    each(0, depth, lambda k: grad.sibling(k, False))
+    for n in range(3, depth):
+        out.send_row(n)
+        out.along(n - 2)
+    grad.send_row(0)
+    each(0, depth, lambda n: grad.sibling(n, False))
+    out.along(depth - 2)
+    grad.send_row(1)
     each(0, depth, grad.keep)
-    each(1, depth, grad.along)
+    for n in range(2, depth):
+        grad.send_row(n)
+        grad.along(n - 2)
     out.result(outputs)
+    grad.along(depth - 2)
     grad.result(grad_tokens)
     out.finish()
     grad.finish()
@@ -383,7 +458,8 @@
     anywhere = pl.BlockSpec(memory_space=pl.ANY)
     dma = pltpu.SemaphoreType.DMA
     weights = pltpu.VMEM((hidden_blocks * slots + 1, block, block), gate_blocks.dtype)
-    gather_sems = [dma((n,)) for n in (depth, depth, depth, depth, 2 * depth, 2 * depth)]
+    gather_sems = [dma((2, depth))]
+    gather_sems += [dma((n,)) for n in (depth, depth, depth, 2 * depth, 2 * depth)]
     thin = jax.ShapeDtypeStruct((hidden_blocks, rows, block), jnp.bfloat16)
     flops = 2 * rows * shard * devices * hidden_blocks * block * 3
     cost = pl.CostEstimate(flops=flops, bytes_accessed=3 * gate_blocks.size * 2, transcendentals=0)
@@ -393,6 +469,7 @@
         in_specs=[vmem] * 2 + [smem] * 3 + [anywhere] * 3,
         out_specs=[vmem] * 3,
         scratch_shapes=[
+            weights,
             weights,
             weights,
             pltpu.VMEM((devices, rows, shard), kind),
@@ -411,9 +488,9 @@
     )(tokens, grad_out, *at, gate_blocks, up_blocks, down_blocks)
     scatter_bufs = [
         pltpu.VMEM((n, rows, shard), jnp.bfloat16)
-        for n in (2 * depth, 2 * depth, depth, depth, depth, depth)
+        for n in (2 * depth, 2 * depth, depth, depth, depth, depth + 1)
     ]
-    scatter_sems = [dma((n,)) for n in (2 * depth, 2 * depth, depth, depth, depth, depth)]
+    scatter_sems = [dma((n,)) for n in (2 * depth, 2 * depth, depth, depth, depth, depth + 1)]
     held = pltpu.VMEM((depth, rows, shard), jnp.float32)
     result = jax.ShapeDtypeStruct((rows, shard), jnp.bfloat16)
     return pl.pallas_call(
@@ -436,10 +513,10 @@
     rows, shard = tokens.shape[0] // dp, tokens.shape[1] // tp
     hidden_blocks, slots = gate_index.shape[0] // tp, gate_index.shape[1]
     block = gate_blocks.shape[-1]
-    held = hidden_blocks * slots * block * block * 2 * 2 + 2 * rows * tokens.shape[1] * 5
+    held = hidden_blocks * slots * block * block * 2 * 3 + 2 * rows * tokens.shape[1] * 3
     return (
         tp % (CORES * ROWS) == 0
-        and tp > CORES * ROWS
+        and tp >= 3 * CORES * ROWS
         and shard % (2 * block) == 0
         and hidden_blocks % 2 == 0
         and rows % 16 == 0

time: 165 us -> 145 us (0.88); the launches traced: 163 us -> 145 us
  Pallas kernels: 156 us -> 138 us
    pallas_call x1, Pallas kernels: 80.1 us -> 69.4 us  [fused_body(): pl.pallas_call(functools.partial(first_kernel, depth, hidden_blocks, slot...]
    pallas_call x1, Pallas kernels: 76.2 us -> 68.6 us  [fused_body(): pl.pallas_call(functools.partial(second_kernel, depth, hidden_blocks, slo...]
where the time goes in v2:
time: 145 us
  Pallas kernels  138 us (95%)
  local copies, waits for them, and re-layouts  3.34 us (2%)
  other arithmetic  3.12 us (2%)
    pallas_call x1, Pallas kernels, fused_body(): pl.pallas_call(functools.partial(first_kernel, depth, hidden_blocks, slot...  69.4 us
    pallas_call x1, Pallas kernels, fused_body(): pl.pallas_call(functools.partial(second_kernel, depth, hidden_blocks, slo...  68.6 us
    unnamed x2, local copies, waits for them, and re-layouts  3.34 us

profile of v2, /device:TPU:0, one launch (start us, length us, event | category | flops | bytes accessed | tf_op | source)
XLA Modules:
  0.0 145.1 jit_solution(3632349932832108228)
XLA Ops:
  0.6 0.8 select_reduce_fusion.2
  1.5 0.9 select_reduce_fusion
  2.4 1.4 add_select_fusion
  3.8 69.4 %gather_and_project.1 = (bf16[8,256,128]{2,1,0:T(8,128)(2,1)}, bf16[8,256,128]{2,1,0:T(8,128)(2,1)}, bf16[8,256,128]{2,1,0:T(8,128)(2,1)}) custom-call(bf16[256,512]{1,0:T(8,128)(2,1)} %refs_0_.1, bf16[256,512]{1,0:T(8,128)(2,1)} %refs_1_.1, s32[8,64]{1,0:T(8,128)} %get-tuple-element.10.refs_2_.refs_3_, s32[8,64]{1,0:T(8,128)} %get-tuple-element.9.refs_3_.refs_4_, ...), custom_call_target="tpu_custom_call" | custom-call | flops 12884901888 | bytes 50331648 | tf_op jit(solution)/shard_map/gather_and_project/pallas_call | solution.py:466
  73.2 68.6 %expand_and_scatter.1 = (bf16[256,512]{1,0:T(8,128)(2,1)}, bf16[256,512]{1,0:T(8,128)(2,1)}) custom-call(bf16[8,256,128]{2,1,0:T(8,128)(2,1)} %get-tuple-element.5.refs_0_, bf16[8,256,128]{2,1,0:T(8,128)(2,1)} %get-tuple-element.6.refs_1_, bf16[8,256,128]{2,1,0:T(8,128)(2,1)} %get-tuple-element.7.refs_2_, s32[8,64]{1,0:T(8,128)} %get-tuple-element.10.refs_2_.refs_3_, ...), custom_call_target="tpu_custom_call" | custom-call | flops 12884901888 | bytes 50331648 | tf_op jit(solution)/shard_map/expand_and_scatter/pallas_call | solution.py:496
  141.8 1.7 %copy.15 = bf16[256,512]{1,0:T(8,128)(2,1)} copy(bf16[256,512]{1,0:T(8,128)(2,1)} %get-tuple-element.15) | data formatting | bytes 524288
  143.5 1.7 %copy.16 = bf16[256,512]{1,0:T(8,128)(2,1)} copy(bf16[256,512]{1,0:T(8,128)(2,1)} %get-tuple-element.16) | data formatting | bytes 524288
  (1 shorter events, 0.0 us)

commit v3 on v2

--- a/solution.py
+++ b/solution.py
@@ -15,12 +15,13 @@
 
 
 def places(index, count):
-    hidden_blocks, slots = index.shape
-    slot = lax.broadcasted_iota(jnp.int32, (hidden_blocks, slots, slots), 1)
-    place = lax.broadcasted_iota(jnp.int32, (hidden_blocks, slots, slots), 2)
-    where = jnp.sum(jnp.where(index[:, :, None] == place, slot, 0), axis=1)
-    base = lax.broadcasted_iota(jnp.int32, (hidden_blocks, slots), 0) * slots
-    return jnp.where(where < count[:, None], base + where, hidden_blocks * slots)
+    weights, hidden_blocks, slots = index.shape
+    cube = (weights, hidden_blocks, slots, slots)
+    slot = lax.broadcasted_iota(jnp.int32, cube, 2)
+    place = lax.broadcasted_iota(jnp.int32, cube, 3)
+    where = jnp.sum(jnp.where(index[..., None] == place, slot, 0), axis=2)
+    base = lax.broadcasted_iota(jnp.int32, index.shape, 1) * slots
+    return jnp.where(where < count[..., None], base + where, hidden_blocks * slots)
 
 
 def position(depth):
@@ -151,107 +152,6 @@
     return lax.dot_general(
         left, right, (((1,), (contract,)), ((), ())), preferred_element_type=jnp.float32
     )
-
-
-def first_kernel(depth, hidden_blocks, slots, block, *refs):
-    (tokens, grads, at_gate, at_up, at_down, gate_hbm, up_hbm, down_hbm) = refs[:8]
-    (hidden, grad_gate, grad_up) = refs[8:11]
-    (first, second, third, all_tokens, all_grads, projected, grad_hidden, load_sems) = refs[11:19]
-    token_sems, grad_sems = refs[19:25], refs[25:31]
-    me = position(depth)[0]
-    per_chip = slots // (depth * ROWS)
-    loads = load_copies(gate_hbm, first, load_sems.at[0], hidden_blocks, slots)
-    loads += load_copies(up_hbm, second, load_sems.at[1], hidden_blocks, slots)
-    down_loads = load_copies(down_hbm, third, load_sems.at[2], hidden_blocks, slots)
-    for load in loads:
-        load.start()
-    all_tokens[me] = tokens[...]
-    all_grads[me] = grads[...]
-    greet(depth)
-    tok = Gather(depth, all_tokens, token_sems)
-    grd = Gather(depth, all_grads, grad_sems)
-    tok.spread(tok.layer)
-    first[hidden_blocks * slots] = jnp.zeros((block, block), first.dtype)
-    second[hidden_blocks * slots] = jnp.zeros((block, block), second.dtype)
-    third[hidden_blocks * slots] = jnp.zeros((block, block), third.dtype)
-    projected[...] = jnp.zeros_like(projected)
-    grad_hidden[...] = jnp.zeros_like(grad_hidden)
-    for load in loads:
-        load.wait()
-    for load in down_loads:
-        load.start()
-
-    def pair(full, chip):
-        return jnp.concatenate([full[CORES * chip + i] for i in range(CORES)], axis=1)
-
-    def project(chip):
-        def one(h):
-            rows = [
-                jnp.concatenate(
-                    [first[at_gate[h, chip * per_chip + j]], second[at_up[h, chip * per_chip + j]]], axis=1
-                )
-                for j in range(per_chip)
-            ]
-            projected[h] += dot(pair(all_tokens, chip), jnp.concatenate(rows, axis=0))
-
-        each(0, hidden_blocks, one)
-
-    def push_back(chip):
-        def one(p):
-            rows = [
-                jnp.concatenate(
-                    [third[at_down[2 * p + i, chip * per_chip + j]] for j in range(per_chip)], axis=1
-                )
-                for i in range(2)
-            ]
-            grad_hidden[p] += dot(pair(all_grads, chip), jnp.concatenate(rows, axis=0), 1)
-
-        each(0, hidden_blocks // 2, one)
-
-    def activate(h):
-        gate, up = projected[h][:, :block], projected[h][:, block:]
-        hidden[h] = (gate * jax.nn.sigmoid(gate) * up).astype(hidden.dtype)
-
-    def arrive(gather, work):
-        gather.from_layer(1)
-        gather.from_row(0)
-        work(gather.chip(0, False))
-
-        def step(i):
-            gather.from_layer(i)
-            gather.from_row(i - 1)
-            work(gather.chip(i - 1, False))
-            work(gather.chip(i - 2, True))
-
-        each(2, depth, step)
-
-    arrive(tok, project)
-    grd.spread(grd.layer)
-    project(tok.chip(depth - 1, False))
-    project(tok.chip(depth - 2, True))
-    tok.from_row(depth - 1)
-    for load in down_loads:
-        load.wait()
-    project(tok.chip(depth - 1, True))
-    arrive(grd, push_back)
-    push_back(grd.chip(depth - 1, False))
-    push_back(grd.chip(depth - 2, True))
-    grd.from_row(depth - 1)
-    each(0, hidden_blocks, activate)
-    push_back(grd.chip(depth - 1, True))
-
-    def back(p):
-        for i in range(2):
-            h = 2 * p + i
-            gate, up = projected[h][:, :block], projected[h][:, block:]
-            flow = grad_hidden[p][:, i * block : (i + 1) * block]
-            sigma = jax.nn.sigmoid(gate)
-            grad_gate[h] = (flow * up * sigma * (1.0 + gate * (1.0 - sigma))).astype(grad_gate.dtype)
-            grad_up[h] = (flow * gate * sigma).astype(grad_up.dtype)
-
-    each(0, hidden_blocks // 2, back)
-    tok.finish()
-    grd.finish()
 
 
 class Scatter:
@@ -359,20 +259,73 @@
             self.z(self.far(n)).wait_send()
 
 
-def second_kernel(depth, hidden_blocks, slots, block, *refs):
-    (hidden, grad_gate, grad_up, at_gate, at_up, at_down, gate_hbm, up_hbm, down_hbm) = refs[:9]
-    (outputs, grad_tokens) = refs[9:11]
-    (first, second, held_out, held_grad, load_sems) = refs[11:16]
-    out_bufs, grad_bufs = refs[16:28], refs[28:40]
-    per_shard = slots // (depth * ROWS * CORES)
-    down_loads = load_copies(down_hbm, first, load_sems.at[0], hidden_blocks, slots)
-    gate_loads = load_copies(gate_hbm, second, load_sems.at[1], hidden_blocks, slots)
-    up_loads = load_copies(up_hbm, first, load_sems.at[2], hidden_blocks, slots)
-    for load in down_loads:
+def layer_kernel(depth, hidden_blocks, slots, block, *refs):
+    tokens, grads, at, gate_hbm, up_hbm, down_hbm, outputs, grad_tokens = refs[:8]
+    (first, second, all_tokens, all_grads, projected, grad_hidden) = refs[8:14]
+    (hidden, grad_gate, grad_up, held_out, held_grad, load_sems) = refs[14:20]
+    token_sems, grad_sems = refs[20:26], refs[26:32]
+    out_bufs, grad_bufs = refs[32:37], refs[37:40]
+    out_sems, back_sems = refs[40:46], refs[46:52]
+    me = position(depth)[0]
+    per_chip = slots // (depth * ROWS)
+    per_shard = per_chip // CORES
+    zero = hidden_blocks * slots
+    gate_loads = load_copies(gate_hbm, first, load_sems.at[0], hidden_blocks, slots)
+    up_loads = load_copies(up_hbm, second, load_sems.at[1], hidden_blocks, slots)
+    down_loads = load_copies(down_hbm, first, load_sems.at[2], hidden_blocks, slots)
+    again_loads = load_copies(gate_hbm, first, load_sems.at[3], hidden_blocks, slots)
+    for load in gate_loads + up_loads:
         load.start()
-    first[hidden_blocks * slots] = jnp.zeros((block, block), first.dtype)
-    second[hidden_blocks * slots] = jnp.zeros((block, block), second.dtype)
+    all_tokens[me] = tokens[...]
+    all_grads[me] = grads[...]
     greet(depth)
+    tok = Gather(depth, all_tokens, token_sems)
+    grd = Gather(depth, all_grads, grad_sems)
+    tok.spread(tok.layer)
+    first[zero] = jnp.zeros((block, block), first.dtype)
+    second[zero] = jnp.zeros((block, block), second.dtype)
+    projected[...] = jnp.zeros_like(projected)
+    grad_hidden[...] = jnp.zeros_like(grad_hidden)
+
+    def pair(full, chip):
+        return jnp.concatenate([full[CORES * chip + i] for i in range(CORES)], axis=1)
+
+    def project(chip):
+        def one(h):
+            rows = [
+                jnp.concatenate(
+                    [first[at[0, h, chip * per_chip + j]], second[at[1, h, chip * per_chip + j]]], axis=1
+                )
+                for j in range(per_chip)
+            ]
+            projected[h] += dot(pair(all_tokens, chip), jnp.concatenate(rows, axis=0))
+
+        each(0, hidden_blocks, one)
+
+    def push_back(chip):
+        def one(p):
+            rows = [
+                jnp.concatenate(
+                    [first[at[2, 2 * p + i, chip * per_chip + j]] for j in range(per_chip)], axis=1
+                )
+                for i in range(2)
+            ]
+            grad_hidden[p] += dot(pair(all_grads, chip), jnp.concatenate(rows, axis=0), 1)
+
+        each(0, hidden_blocks // 2, one)
+
+    def activate(h):
+        gate, up = projected[h][:, :block], projected[h][:, block:]
+        hidden[h] = (gate * jax.nn.sigmoid(gate) * up).astype(hidden.dtype)
+
+    def back(p):
+        for i in range(2):
+            h = 2 * p + i
+            gate, up = projected[h][:, :block], projected[h][:, block:]
+            flow = grad_hidden[p][:, i * block : (i + 1) * block]
+            sigma = jax.nn.sigmoid(gate)
+            grad_gate[h] = (flow * up * sigma * (1.0 + gate * (1.0 - sigma))).astype(grad_gate.dtype)
+            grad_up[h] = (flow * gate * sigma).astype(grad_up.dtype)
 
     def wide(ref):
         return jnp.concatenate([ref[h] for h in range(hidden_blocks)], axis=1)
@@ -382,7 +335,7 @@
         for j in range(0, per_shard, 2):
             place = shard * per_shard + j
             rows = [
-                jnp.concatenate([first[at_down[h, place + i]] for i in range(2)], axis=1)
+                jnp.concatenate([first[at[2, h, place + i]] for i in range(2)], axis=1)
                 for h in range(hidden_blocks)
             ]
             value = dot(wide(hidden), jnp.concatenate(rows, axis=0))
@@ -394,9 +347,9 @@
         for j in range(0, per_shard, 2):
             place = shard * per_shard + j
             value = None
-            for left, buffer, at in ((grad_gate, second, at_gate), (grad_up, first, at_up)):
+            for left, buffer, kind in ((grad_gate, first, 0), (grad_up, second, 1)):
                 rows = [
-                    jnp.concatenate([buffer[at[h, place + i]] for h in range(hidden_blocks)], axis=1)
+                    jnp.concatenate([buffer[at[kind, h, place + i]] for h in range(hidden_blocks)], axis=1)
                     for i in range(2)
                 ]
                 term = dot(wide(left), jnp.concatenate(rows, axis=0), 1)
@@ -404,21 +357,60 @@
             parts.append((slice(j * block, (j + 2) * block), value))
         return parts
 
-    out = Scatter(depth, out_partial, held_out, out_bufs)
-    grad = Scatter(depth, grad_partial, held_grad, grad_bufs)
+    def arrive(gather, work, loads):
+        gather.from_layer(1)
+        gather.from_row(0)
+        for load in loads:
+            load.wait()
+        work(gather.chip(0, False))
+
+        def step(i):
+            gather.from_layer(i)
+            gather.from_row(i - 1)
+            work(gather.chip(i - 1, False))
+            work(gather.chip(i - 2, True))
+
+        each(2, depth, step)
+
+    last = depth - 1
+    arrive(tok, project, gate_loads + up_loads)
+    grd.spread(grd.layer)
+    project(tok.chip(last, False))
+    project(tok.chip(last - 1, True))
+    tok.from_row(last)
+    project(tok.chip(last, True))
     for load in down_loads:
-        load.wait()
-    for load in gate_loads:
         load.start()
+    each(0, hidden_blocks, activate)
+    arrive(grd, push_back, down_loads)
+
+    tok.finish()
+    out_stage = (all_tokens.at[pl.ds(0, 2 * depth)],) + out_bufs
+    back_stage = (
+        all_tokens.at[pl.ds(2 * depth, 2 * depth)],
+        grad_bufs[0],
+        all_grads.at[pl.ds(0, depth)],
+        grad_bufs[1],
+        all_grads.at[pl.ds(depth, depth)],
+        grad_bufs[2],
+    )
+    out = Scatter(depth, out_partial, held_out, out_stage + out_sems)
+    grad = Scatter(depth, grad_partial, held_grad, back_stage + back_sems)
     each(0, depth, lambda n: out.sibling(n, True))
+    push_back(grd.chip(last, False))
+    push_back(grd.chip(last - 1, True))
     each(0, depth, out.across)
     out.send_row(0)
+    each(0, depth, lambda n: out.sibling(n, False))
+    grd.from_row(last)
     out.send_row(1)
-    each(0, depth, lambda n: out.sibling(n, False))
     each(0, depth, out.keep)
-    for load in up_loads:
+    push_back(grd.chip(last, True))
+    for load in again_loads:
         load.start()
-    for load in gate_loads + up_loads:
+    each(0, hidden_blocks // 2, back)
+    grd.finish()
+    for load in again_loads:
         load.wait()
     each(0, depth, lambda n: grad.sibling(n, True))
     out.send_row(2)
@@ -447,12 +439,9 @@
     block = gate_blocks.shape[-1]
     rows, shard = tokens.shape
     devices = depth * ROWS * CORES
-    kind = tokens.dtype
-    at = [
-        places(gate_index, gate_count),
-        places(up_index, up_count),
-        places(down_index, down_count),
-    ]
+    at = places(
+        jnp.stack([gate_index, up_index, down_index]), jnp.stack([gate_count, up_count, down_count])
+    )
     vmem = pl.BlockSpec(memory_space=pltpu.VMEM)
     smem = pl.BlockSpec(memory_space=pltpu.SMEM)
     anywhere = pl.BlockSpec(memory_space=pl.ANY)
@@ -460,52 +449,43 @@
     weights = pltpu.VMEM((hidden_blocks * slots + 1, block, block), gate_blocks.dtype)
     gather_sems = [dma((2, depth))]
     gather_sems += [dma((n,)) for n in (depth, depth, depth, 2 * depth, 2 * depth)]
-    thin = jax.ShapeDtypeStruct((hidden_blocks, rows, block), jnp.bfloat16)
-    flops = 2 * rows * shard * devices * hidden_blocks * block * 3
-    cost = pl.CostEstimate(flops=flops, bytes_accessed=3 * gate_blocks.size * 2, transcendentals=0)
-    hidden, grad_gate, grad_up = pl.pallas_call(
-        functools.partial(first_kernel, depth, hidden_blocks, slots, block),
-        out_shape=[thin] * 3,
-        in_specs=[vmem] * 2 + [smem] * 3 + [anywhere] * 3,
-        out_specs=[vmem] * 3,
+    scatter_sems = [dma((n,)) for n in (2 * depth, 2 * depth, depth, depth, depth, depth + 1)]
+    thin = pltpu.VMEM((hidden_blocks, rows, block), jnp.bfloat16)
+    held = pltpu.VMEM((depth, rows, shard), jnp.float32)
+    full = pltpu.VMEM((devices, rows, shard), tokens.dtype)
+    sizes = (2 * depth, depth, depth, depth, depth + 1, 2 * depth, depth, depth + 1)
+    result = jax.ShapeDtypeStruct((rows, shard), jnp.bfloat16)
+    flops = 2 * rows * shard * devices * hidden_blocks * block * 6
+    return pl.pallas_call(
+        functools.partial(layer_kernel, depth, hidden_blocks, slots, block),
+        out_shape=[result] * 2,
+        in_specs=[vmem] * 2 + [smem] + [anywhere] * 3,
+        out_specs=[vmem] * 2,
         scratch_shapes=[
             weights,
             weights,
-            weights,
-            pltpu.VMEM((devices, rows, shard), kind),
-            pltpu.VMEM((devices, rows, shard), kind),
+            full,
+            full,
             pltpu.VMEM((hidden_blocks, rows, 2 * block), jnp.float32),
             pltpu.VMEM((hidden_blocks // 2, rows, 2 * block), jnp.float32),
-            dma((3, hidden_blocks)),
+            thin,
+            thin,
+            thin,
+            held,
+            held,
+            dma((4, hidden_blocks)),
         ]
-        + gather_sems
-        + gather_sems,
+        + gather_sems * 2
+        + [pltpu.VMEM((n, rows, shard), jnp.bfloat16) for n in sizes]
+        + scatter_sems * 2,
         compiler_params=pltpu.CompilerParams(
             collective_id=0, has_side_effects=True, vmem_limit_bytes=VMEM_LIMIT
         ),
-        cost_estimate=cost,
-        name="gather_and_project",
-    )(tokens, grad_out, *at, gate_blocks, up_blocks, down_blocks)
-    scatter_bufs = [
-        pltpu.VMEM((n, rows, shard), jnp.bfloat16)
-        for n in (2 * depth, 2 * depth, depth, depth, depth, depth + 1)
-    ]
-    scatter_sems = [dma((n,)) for n in (2 * depth, 2 * depth, depth, depth, depth, depth + 1)]
-    held = pltpu.VMEM((depth, rows, shard), jnp.float32)
-    result = jax.ShapeDtypeStruct((rows, shard), jnp.bfloat16)
-    return pl.pallas_call(
-        functools.partial(second_kernel, depth, hidden_blocks, slots, block),
-        out_shape=[result] * 2,
-        in_specs=[vmem] * 3 + [smem] * 3 + [anywhere] * 3,
-        out_specs=[vmem] * 2,
-        scratch_shapes=[weights, weights, held, held, dma((3, hidden_blocks))]
-        + (scatter_bufs + scatter_sems) * 2,
-        compiler_params=pltpu.CompilerParams(
-            collective_id=1, has_side_effects=True, vmem_limit_bytes=VMEM_LIMIT
+        cost_estimate=pl.CostEstimate(
+            flops=flops, bytes_accessed=4 * gate_blocks.size * 2, transcendentals=0
         ),
-        cost_estimate=cost,
-        name="expand_and_scatter",
-    )(hidden, grad_gate, grad_up, *at, gate_blocks, up_blocks, down_blocks)
+        name="block_pruned_layer",
+    )(tokens, grad_out, at, gate_blocks, up_blocks, down_blocks)
 
 
 def fits(mesh, tokens, gate_index, gate_blocks):
@@ -513,7 +493,7 @@
     rows, shard = tokens.shape[0] // dp, tokens.shape[1] // tp
     hidden_blocks, slots = gate_index.shape[0] // tp, gate_index.shape[1]
     block = gate_blocks.shape[-1]
-    held = hidden_blocks * slots * block * block * 2 * 3 + 2 * rows * tokens.shape[1] * 3
+    held = hidden_blocks * slots * block * block * 2 * 2 + 2 * rows * tokens.shape[1] * 6
     return (
         tp % (CORES * ROWS) == 0
         and tp >= 3 * CORES * ROWS

time: 145 us -> 137 us (0.945)
  Pallas kernels: 138 us -> 130 us
    pallas_call x2 -> x1, Pallas kernels: 138 us -> 130 us  [fused_body(): pl.pallas_call(functools.partial(layer_kernel, depth, hidden_blocks, slot...]
    reduce_sum x2 -> x1, other arithmetic: 1.75 us -> 0.29 us  [places(): where = jnp.sum(jnp.where(index[..., None] == place, slot, 0), axis=2)]
where the time goes in v3:
time: 137 us; the launch traced here: 136 us
  Pallas kernels  130 us (95%)
  local copies, waits for them, and re-layouts  3.34 us (2%)
  other arithmetic  2.38 us (2%)
    pallas_call x1, Pallas kernels, fused_body(): pl.pallas_call(functools.partial(layer_kernel, depth, hidden_blocks, slot...  130 us
    unnamed x2, local copies, waits for them, and re-layouts  3.34 us

profile of v3, /device:TPU:0, one launch (start us, length us, event | category | flops | bytes accessed | tf_op | source)
XLA Modules:
  0.0 136.5 jit_solution(6197951076131436122)
XLA Ops:
  0.6 0.7 pad_add_fusion.1
  1.3 0.7 pad_add_fusion
  2.1 0.3 select_reduce_fusion
  2.4 0.7 add_select_fusion.refs_2_
  3.0 130.1 %block_pruned_layer.1 = (bf16[256,512]{1,0:T(8,128)(2,1)}, bf16[256,512]{1,0:T(8,128)(2,1)}) custom-call(bf16[256,512]{1,0:T(8,128)(2,1)} %refs_0_.1, bf16[256,512]{1,0:T(8,128)(2,1)} %refs_1_.1, s32[3,8,64]{2,1,0:T(8,128)} %add_select_fusion.refs_2_, bf16[512,128,128]{2,1,0:T(8,128)(2,1)} %refs_3_.1, bf16[512,128,128]{2,1,0:T(8,128)(2,1)} %refs_4_.1, ...), custom_call_target="tpu_custom_call" | custom-call | flops 25769803776 | bytes 67108864 | tf_op jit(solution)/shard_map/block_pruned_layer/pallas_call | solution.py:459
  133.1 1.7 %copy.15 = bf16[256,512]{1,0:T(8,128)(2,1)} copy(bf16[256,512]{1,0:T(8,128)(2,1)} %get-tuple-element.4) | data formatting | bytes 524288
  134.8 1.7 %copy.16 = bf16[256,512]{1,0:T(8,128)(2,1)} copy(bf16[256,512]{1,0:T(8,128)(2,1)} %get-tuple-element.5) | data formatting | bytes 524288
  (1 shorter events, 0.0 us)

commit v4 on v3

--- a/solution.py
+++ b/solution.py
@@ -206,9 +206,10 @@
             total = value + self.c_in[layer, :, cols].astype(jnp.float32)
             self.y_out[layer, :, cols] = total.astype(self.y_out.dtype)
 
+    def hold_row(self, n):
+        self.y(n - 2).wait_send()
+
     def send_row(self, n):
-        if n >= 2:
-            self.y(n - 2).wait_send()
         self.y(n).start()
 
     def keep(self, n):
@@ -250,10 +251,10 @@
 
         out[...] = self.held[mine].astype(out.dtype)
 
-    def finish(self):
+    def finish(self, held):
         for i in range(2 * self.depth):
             self.c(i).wait_send()
-        for n in range(max(self.depth - 2, 0), self.depth):
+        for n in range(held, self.depth):
             self.y(n).wait_send()
         for n in range(self.depth - 1):
             self.z(self.far(n)).wait_send()
@@ -357,32 +358,44 @@
             parts.append((slice(j * block, (j + 2) * block), value))
         return parts
 
-    def arrive(gather, work, loads):
-        gather.from_layer(1)
-        gather.from_row(0)
-        for load in loads:
-            load.wait()
-        work(gather.chip(0, False))
-
-        def step(i):
-            gather.from_layer(i)
-            gather.from_row(i - 1)
-            work(gather.chip(i - 1, False))
-            work(gather.chip(i - 2, True))
-
-        each(2, depth, step)
-
     last = depth - 1
-    arrive(tok, project, gate_loads + up_loads)
+    tok.from_layer(1)
+    tok.from_row(0)
+    for load in gate_loads + up_loads:
+        load.wait()
+    project(tok.chip(0, False))
+
+    def token_step(i):
+        tok.from_layer(i)
+        tok.from_row(i - 1)
+        project(tok.chip(i - 1, False))
+        project(tok.chip(i - 2, True))
+
+    each(2, depth, token_step)
     grd.spread(grd.layer)
     project(tok.chip(last, False))
     project(tok.chip(last - 1, True))
+    grd.from_layer(1)
     tok.from_row(last)
+    grd.from_row(0)
     project(tok.chip(last, True))
     for load in down_loads:
         load.start()
+    grd.from_layer(2)
+    grd.from_row(1)
     each(0, hidden_blocks, activate)
-    arrive(grd, push_back, down_loads)
+    for load in down_loads:
+        load.wait()
+    push_back(grd.chip(0, False))
+    push_back(grd.chip(0, True))
+
+    def grad_step(i):
+        grd.from_layer(i)
+        grd.from_row(i - 1)
+        push_back(grd.chip(i - 2, False))
+        push_back(grd.chip(i - 2, True))
+
+    each(3, depth, grad_step)
 
     tok.finish()
     out_stage = (all_tokens.at[pl.ds(0, 2 * depth)],) + out_bufs
@@ -397,41 +410,40 @@
     out = Scatter(depth, out_partial, held_out, out_stage + out_sems)
     grad = Scatter(depth, grad_partial, held_grad, back_stage + back_sems)
     each(0, depth, lambda n: out.sibling(n, True))
+    push_back(grd.chip(last - 1, False))
+    push_back(grd.chip(last - 1, True))
     push_back(grd.chip(last, False))
-    push_back(grd.chip(last - 1, True))
     each(0, depth, out.across)
-    out.send_row(0)
+    each(0, depth, out.send_row)
     each(0, depth, lambda n: out.sibling(n, False))
     grd.from_row(last)
-    out.send_row(1)
     each(0, depth, out.keep)
     push_back(grd.chip(last, True))
     for load in again_loads:
         load.start()
     each(0, hidden_blocks // 2, back)
     grd.finish()
+    out.along(0)
     for load in again_loads:
         load.wait()
     each(0, depth, lambda n: grad.sibling(n, True))
-    out.send_row(2)
-    out.along(0)
     each(0, depth, grad.across)
-    for n in range(3, depth):
-        out.send_row(n)
-        out.along(n - 2)
     grad.send_row(0)
+    grad.send_row(1)
+    out.along(1)
     each(0, depth, lambda n: grad.sibling(n, False))
-    out.along(depth - 2)
-    grad.send_row(1)
+    for n in range(2, depth - 1):
+        out.along(n)
     each(0, depth, grad.keep)
     for n in range(2, depth):
+        grad.hold_row(n)
         grad.send_row(n)
         grad.along(n - 2)
     out.result(outputs)
     grad.along(depth - 2)
     grad.result(grad_tokens)
-    out.finish()
-    grad.finish()
+    out.finish(0)
+    grad.finish(depth - 2)
 
 
 def fused_body(depth, tokens, grad_out, gate_blocks, gate_index, gate_count, up_blocks, up_index, up_count, down_blocks, down_index, down_count):

time: 137 us -> 133 us (0.971)
  Pallas kernels: 130 us -> 127 us
    pallas_call x1, Pallas kernels: 130 us -> 127 us  [fused_body(): pl.pallas_call(functools.partial(layer_kernel, depth, hidden_blocks, slot...]
where the time goes in v4:
time: 133 us
  Pallas kernels  127 us (95%)
  local copies, waits for them, and re-layouts  3.34 us (3%)
  other arithmetic  2.38 us (2%)
    pallas_call x1, Pallas kernels, fused_body(): pl.pallas_call(functools.partial(layer_kernel, depth, hidden_blocks, slot...  127 us
    unnamed x2, local copies, waits for them, and re-layouts  3.34 us

profile of v4, /device:TPU:0, one launch (start us, length us, event | category | flops | bytes accessed | tf_op | source)
XLA Modules:
  0.0 132.9 jit_solution(16535752509721271133)
XLA Ops:
  0.6 0.7 pad_add_fusion.1
  1.3 0.7 pad_add_fusion
  2.1 0.3 select_reduce_fusion
  2.4 0.7 add_select_fusion.refs_2_
  3.0 126.5 %block_pruned_layer.1 = (bf16[256,512]{1,0:T(8,128)(2,1)}, bf16[256,512]{1,0:T(8,128)(2,1)}) custom-call(bf16[256,512]{1,0:T(8,128)(2,1)} %refs_0_.1, bf16[256,512]{1,0:T(8,128)(2,1)} %refs_1_.1, s32[3,8,64]{2,1,0:T(8,128)} %add_select_fusion.refs_2_, bf16[512,128,128]{2,1,0:T(8,128)(2,1)} %refs_3_.1, bf16[512,128,128]{2,1,0:T(8,128)(2,1)} %refs_4_.1, ...), custom_call_target="tpu_custom_call" | custom-call | flops 25769803776 | bytes 67108864 | tf_op jit(solution)/shard_map/block_pruned_layer/pallas_call | solution.py:471
  129.6 1.7 %copy.15 = bf16[256,512]{1,0:T(8,128)(2,1)} copy(bf16[256,512]{1,0:T(8,128)(2,1)} %get-tuple-element.4) | data formatting | bytes 524288
  131.2 1.7 %copy.16 = bf16[256,512]{1,0:T(8,128)(2,1)} copy(bf16[256,512]{1,0:T(8,128)(2,1)} %get-tuple-element.5) | data formatting | bytes 524288
  (1 shorter events, 0.0 us)
